TPU v7x, 128 devices: a whole 4x4x4 slice. The times are simulated.
128 devices in a mesh: ctx: 16 (over y_lo, z, core), head: 8 (over x, y_hi).
Axes of the slice: x: 4, y: 4 (y_hi: 2, y_lo: 2; y = y_hi * 2 + y_lo), z: 4, core: 2. Of those that a mesh axis runs over, the one named last changes fastest.
Arguments:
- queries: bfloat16 [2048, 36864], P('ctx', 'head'), may hold values from -296 to 296
- latent_keys: bfloat16 [2048, 576], P('ctx'), may hold values from -9 to 9
- block_order: int32 [16], replicated, may hold values from 0 to 15, each once
- out_grad: bfloat16 [2048, 32768], P('ctx', 'head'), may hold values from -6 to 6
Outputs:
- attended: bfloat16 [2048, 32768], P('ctx', 'head')
- query_grad: bfloat16 [2048, 36864], P('ctx', 'head')
- latent_grad: bfloat16 [2048, 576], P('ctx')
Inputs may be any that keep to these rules, and one draw needn't show every extreme that they name: `block_order`: a permutation: each block index once.
All inputs are finite; a program needn't handle non-finite values.
Results may differ from a plain program's by a relative error of at most 0.034.
Values may be sent and summed in bfloat16 or wider, within the bound.
A program may use at most 64 MiB of HBM per device.

v0:
```python
import jax
import jax.numpy as jnp
from jax import lax
from jax.sharding import PartitionSpec as P

LATENT = 512
ROPE = 64


score_scale = 192.0 ** (-0.5)
masked_value = -1e30


def row_positions(block_order, first_row, count, shard_rows):
    rows = first_row + jnp.arange(count, dtype=jnp.int32)
    owner = rows // shard_rows
    blocks = block_order.shape[0]
    onehot = (owner[:, None] == jnp.arange(blocks, dtype=jnp.int32)[None, :]).astype(jnp.int32)
    base = jnp.sum(onehot * block_order[None, :], axis=1)
    return base * shard_rows + rows % shard_rows


def local(queries, latent_keys, block_order, out_grad):
    kdim = LATENT + ROPE
    shard_rows = latent_keys.shape[0]
    head_count = queries.shape[1] // kdim
    query_three = queries.reshape(shard_rows, head_count, kdim)
    grad_three = out_grad.reshape(shard_rows, head_count, LATENT)
    own_index = lax.axis_index("ctx")
    query_pos = row_positions(block_order, own_index * shard_rows, shard_rows, shard_rows)

    def piece_scores(piece, start):
        score = (
            jnp.einsum("thd,pd->htp", query_three, piece, preferred_element_type=jnp.float32)
            * score_scale
        )
        key_pos = row_positions(block_order, start, piece.shape[0], shard_rows)
        visible = key_pos[None, :] <= query_pos[:, None]
        return (jnp.where(visible[None], score, masked_value), visible)

    running_max = jnp.full((head_count, shard_rows), masked_value, jnp.float32)
    score, visible = piece_scores(
        lax.all_gather(latent_keys, "ctx", axis=0, tiled=True), jnp.int32(0)
    )
    new_max = jnp.maximum(running_max, jnp.max(score, axis=2))
    weights = jnp.where(visible[None], jnp.exp(score - new_max[:, :, None]), 0.0)
    new_sum = jnp.sum(weights, axis=2)
    lse = new_max + jnp.log(new_sum)
    piece = lax.all_gather(latent_keys, "ctx", axis=0, tiled=True)
    score, visible = piece_scores(piece, jnp.int32(0))
    prob_b = jnp.where(visible[None], jnp.exp(score - lse[:, :, None]), 0.0).astype(jnp.bfloat16)
    accum = jnp.einsum("htp,pe->the", prob_b, piece[:, :LATENT], preferred_element_type=jnp.float32)
    attended = accum.astype(jnp.bfloat16)
    delta = jnp.sum(attended.astype(jnp.float32) * grad_three.astype(jnp.float32), axis=2).T
    piece = lax.all_gather(latent_keys, "ctx", axis=0, tiled=True)
    score, visible = piece_scores(piece, jnp.int32(0))
    prob = jnp.where(visible[None], jnp.exp(score - lse[:, :, None]), 0.0)
    prob_b = prob.astype(jnp.bfloat16)
    dprob = jnp.einsum(
        "the,pe->htp", grad_three, piece[:, :LATENT], preferred_element_type=jnp.float32
    )
    dscore = (prob * (dprob - delta[:, :, None])).astype(jnp.bfloat16)
    query_accum = jnp.einsum("htp,pd->thd", dscore, piece, preferred_element_type=jnp.float32)
    key_part = score_scale * jnp.einsum(
        "htp,thd->pd", dscore, query_three, preferred_element_type=jnp.float32
    )
    value_part = jnp.einsum("htp,the->pe", prob_b, grad_three, preferred_element_type=jnp.float32)
    term = key_part + jnp.pad(value_part, ((0, 0), (0, ROPE)))
    key_accum = term
    query_accum, key_accum = (query_accum, key_accum)
    query_grad = (
        (score_scale * query_accum).astype(jnp.bfloat16).reshape(shard_rows, head_count * kdim)
    )
    partial_rows = lax.psum_scatter(key_accum, "ctx", scatter_dimension=0, tiled=True)
    latent_grad = lax.psum(partial_rows, "head").astype(jnp.bfloat16)
    return (attended.reshape(shard_rows, head_count * LATENT), query_grad, latent_grad)


def solution(mesh):
    placed = (P("ctx", "head"), P("ctx", None), P(), P("ctx", "head"))
    return jax.shard_map(
        local,
        mesh=mesh,
        in_specs=placed,
        out_specs=(P("ctx", "head"), P("ctx", "head"), P("ctx", None)),
        check_vma=False,
    )
```

profile of v0, /device:TPU:0, one launch (start us, length us, event | category | flops | bytes accessed | tf_op | source)
XLA Modules:
  0.0 196.5 jit_solution(11976603212448171671)
XLA Ops:
  7.2 0.0 copy-start
  7.2 0.0 copy-start.3
  7.2 0.0 all-gather.2.cloned.1.call-start
  7.2 0.7 all-gather.2.cloned.1.call-update
  7.9 0.0 reduce-scatter.2.cloned.1.call-start
  8.0 1.6 copy.34
  9.6 1.3 copy.37
  10.9 0.0 copy-done
  10.9 0.7 copy.30
  11.7 0.0 copy-done.3
  11.7 0.1 select_reduce_fusion.2
  11.8 0.1 select_reduce_fusion.1
  11.9 0.3 broadcast_compare_fusion
  12.2 38.2 %all-gather.2.cloned.1.call-done = bf16[2048,576]{0,1:T(8,128)(2,1)} async-done(((bf16[128,576]{0,1:T(8,128)(2,1)}), bf16[2048,576]{0,1:T(8,128)(2,1)}) %all-gather.2.cloned.1.call-update) | async-done | bytes 2359312 | tf_op jit(solution)/shard_map/all_gather | solution.py:49
  50.5 5.6 %fusion.3 = (f32[8,128]{1,0:T(8,128)S(1)}, f32[2048,128,8]{1,0,2:T(8,128)S(1)}) fusion(pred[128,2048]{0,1:T(8,128)(4,1)S(1)} %broadcast_compare_fusion, bf16[128,8,576]{0,2,1:T(8,128)(2,1)S(1)} %bitcast.65, bf16[2048,576]{0,1:T(8,128)(2,1)} %all-gather.2.cloned.1.call-done), kind=kOutput, calls=%fused_computation.7 | convolution fusion | flops 2422209536 | bytes 12193792 | tf_op jit(solution)/shard_map/thd,pd->htp/dot_general | solution.py:34
  56.1 2.0 %select_reduce_fusion = f32[8,128]{1,0:T(8,128)S(1)} fusion(f32[2048,128,8]{1,0,2:T(8,128)S(1)} %get-tuple-element.13, f32[8,128]{1,0:T(8,128)S(1)} %broadcast_maximum_fusion, pred[128,2048]{0,1:T(8,128)(4,1)S(1)} %broadcast_compare_fusion), kind=kLoop, calls=%fused_computation.5 | loop fusion | flops 10484736 | bytes 8658944 | tf_op jit(solution)/shard_map/reduce_sum | solution.py:47
  58.1 0.0 copy-start.1
  58.2 0.0 copy-start.4
  58.2 2.7 %convolution_bitcast_fusion = f32[2048,512]{0,1:T(8,128)S(1)} fusion(bf16[128,8,512]{0,2,1:T(8,128)(2,1)S(1)} %bitcast.62, f32[2048,128,8]{1,0,2:T(8,128)S(1)} %get-tuple-element.13, f32[8,128]{1,0:T(8,128)S(1)} %log_add_fusion, pred[128,2048]{0,1:T(8,128)(4,1)S(1)} %broadcast_compare_fusion), kind=kOutput, calls=%fused_computation.10 | convolution fusion | flops 2157969408 | bytes 13897728 | tf_op jit(solution)/shard_map/htp,the->pe/dot_general | solution.py:67
  60.9 0.0 copy-done.1
  60.9 0.0 copy-done.4
  60.9 3.7 %multiply_reduce_fusion = (f32[128,8]{0,1:T(8,128)S(1)}, bf16[128,8,512]{2,0,1:T(8,128)(2,1)}) fusion(bf16[128,8,512]{2,0,1:T(8,128)(2,1)S(1)} %copy-done.1, bf16[2048,576]{0,1:T(8,128)(2,1)S(1)} %copy-done.4, f32[2048,128,8]{1,0,2:T(8,128)S(1)} %get-tuple-element.13, f32[8,128]{1,0:T(8,128)S(1)} %log_add_fusion, ...), kind=kOutput, calls=%fused_computation.17 | convolution fusion | flops 2160589824 | bytes 12853248 | tf_op jit(solution)/shard_map/htp,pe->the/dot_general | solution.py:52
  64.6 4.5 %fusion.1 = bf16[8,128,2048]{1,2,0:T(8,128)(2,1)S(1)} fusion(f32[2048,128,8]{1,0,2:T(8,128)S(1)} %get-tuple-element.13, bf16[128,8,512]{0,2,1:T(8,128)(2,1)S(1)} %bitcast.63, f32[8,128]{1,0:T(8,128)S(1)} %bitcast.68, f32[8,128]{1,0:T(8,128)S(1)} %log_add_fusion, pred[128,2048]{0,1:T(8,128)(4,1)S(1)} %broadcast_compare_fusion, bf16[2048,576]{0,1:T(8,128)(2,1)S(1)} %copy-done.4), kind=kOutput, calls=%fused_computation.2 | convolution fusion | flops 2162163712 | bytes 15998976 | tf_op jit(solution)/shard_map/the,pe->htp/dot_general | solution.py:59
  69.0 0.0 copy-start.5
  69.0 2.0 %copy-done.5 = bf16[8,128,2048]{1,2,0:T(8,128)(2,1)} copy-done((bf16[8,128,2048]{1,2,0:T(8,128)(2,1)}, bf16[8,128,2048]{1,2,0:T(8,128)(2,1)S(1)}, u32[]{:S(2)}) %copy-start.5) | copy-done | bytes 4194328
  71.0 4.3 %fusion.4 = f32[2048,576]{0,1:T(8,128)} fusion(f32[2048,512]{0,1:T(8,128)S(1)} %convolution_bitcast_fusion, bf16[8,128,2048]{1,2,0:T(8,128)(2,1)S(1)} %fusion.1, bf16[128,8,576]{0,2,1:T(8,128)(2,1)S(1)} %bitcast.66), kind=kOutput, calls=%fused_computation.9 | convolution fusion | flops 2418278400 | bytes 14286848 | tf_op jit(solution)/shard_map/htp,thd->pd/dot_general | solution.py:64
  75.4 0.0 copy-start.2
  75.4 0.0 reduce-scatter.2.cloned.1.call-update
  75.4 1.2 copy-done.2
  76.6 0.7 copy.33
  77.2 1.3 copy.41
  78.6 5.5 %multiply_convert_fusion = bf16[8,128,576]{1,2,0:T(8,128)(2,1)S(1)} fusion(bf16[8,128,2048]{1,2,0:T(8,128)(2,1)} %copy-done.5, bf16[2048,576]{0,1:T(8,128)(2,1)} %all-gather.2.cloned.1.call-done), kind=kOutput, calls=%fused_computation.15 | convolution fusion | flops 2417098752 | bytes 7733248 | tf_op jit(solution)/shard_map/htp,pd->thd/dot_general | solution.py:63
  84.1 1.4 copy.42
  85.5 58.2 %reduce-scatter.2.cloned.1.call-done = f32[128,576]{0,1:T(8,128)} async-done(((f32[2048,576]{0,1:T(8,128)}), f32[128,576]{0,1:T(8,128)}) %reduce-scatter.2.cloned.1.call-update) | async-done | bytes 294928 | tf_op jit(solution)/shard_map/reduce_scatter | solution.py:74
  143.7 45.9 %all-reduce.2 = bf16[128,576]{0,1:T(8,128)(2,1)} all-reduce(f32[128,576]{0,1:T(8,128)} %reduce-scatter.2.cloned.1.call-done), channel_id=1, replica_groups=mesh['ctx'=16,'head'=8] {'head'}, use_global_device_ids=true, to_apply=%region_6.7 | all-reduce | flops 73728 | bytes 442368 | tf_op jit(solution)/shard_map/psum | solution.py:75
  (6 shorter events, 0.0 us)
Async XLA Ops:
  7.2 3.7 %copy-start = (bf16[128,4608]{1,0:T(8,128)(2,1)S(1)}, bf16[128,4608]{1,0:T(8,128)(2,1)}, u32[]{:S(2)}) copy-start(bf16[128,4608]{1,0:T(8,128)(2,1)} %param.4) | copy-start | bytes 3538948
  7.2 4.5 %copy-start.3 = (s32[16]{0:T(128)S(1)}, s32[16]{0:T(128)}, u32[]{:S(2)}) copy-start(s32[16]{0:T(128)} %param.6) | copy-start | bytes 196
  7.2 43.3 %all-gather.2.cloned.1.call-start = ((), (), s32[]{:S(2)}) async-start(), calls=%async_computation.1 | async-start | bytes 2506752 | tf_op jit(solution)/shard_map/all_gather | solution.py:49
  7.9 135.8 %reduce-scatter.2.cloned.1.call-start = ((), (), s32[]{:S(2)}) async-start(), calls=%async_computation.2 | async-start | bytes 5013504 | tf_op jit(solution)/shard_map/reduce_scatter | solution.py:74
  58.1 2.7 %copy-start.1 = (bf16[128,8,512]{2,0,1:T(8,128)(2,1)S(1)}, bf16[128,8,512]{2,0,1:T(8,128)(2,1)}, u32[]{:S(2)}) copy-start(bf16[128,8,512]{2,0,1:T(8,128)(2,1)} %copy.37) | copy-start | bytes 3145732
  58.2 2.7 %copy-start.4 = (bf16[2048,576]{0,1:T(8,128)(2,1)S(1)}, bf16[2048,576]{0,1:T(8,128)(2,1)}, u32[]{:S(2)}) copy-start(bf16[2048,576]{0,1:T(8,128)(2,1)} %all-gather.2.cloned.1.call-done) | copy-start | bytes 7077892
  69.0 2.0 %copy-start.5 = (bf16[8,128,2048]{1,2,0:T(8,128)(2,1)}, bf16[8,128,2048]{1,2,0:T(8,128)(2,1)S(1)}, u32[]{:S(2)}) copy-start(bf16[8,128,2048]{1,2,0:T(8,128)(2,1)S(1)} %fusion.1) | copy-start | bytes 12582916
  75.4 1.2 copy-start.2
Sparse Core Ops, SparseCore 0:
  9.6 40.7 all-gather.1
  75.5 68.1 reduce-scatter.1
where the time goes:
time: 197 us; the launch traced here: 196 us
  waiting for transfers between devices  97.2 us (49%)
  blocking collectives  45.9 us (23%)
  matrix products  26.2 us (13%)
  between operations  14.2 us (7%)
  local copies, waits for them, and re-layouts  10.3 us (5%)
  other arithmetic  2.6 us (1%)
    reduce_scatter x1, waiting for transfers between devices, local(): lax.psum_scatter(key_accum, 'ctx', scatter_dimension=0, tiled=True)  58.2 us
    psum x1, blocking collectives, local(): latent_grad = lax.psum(partial_rows, 'head').astype(jnp.bfloat16)  45.9 us
    all_gather x1, waiting for transfers between devices, local(): piece = lax.all_gather(latent_keys, 'ctx', axis=0, tiled=True)  38.2 us
    unnamed x16, local copies, waits for them, and re-layouts  8.29 us
    dot_general x1, matrix products, piece_scores(): jnp.einsum('thd,pd->htp', query_three, piece, preferred_element_type=jnp....  5.59 us
    dot_general x1, matrix products, local(): jnp.einsum('htp,pd->thd', dscore, piece, preferred_element_type=jnp.float32)  5.5 us
    dot_general x1, matrix products, local(): jnp.einsum('the,pe->htp', grad_three, piece[:, :LATENT], preferred_elemen...  4.47 us
    dot_general x1, matrix products, local(): jnp.einsum('htp,thd->pd', dscore, query_three, preferred_element_type=jnp...  4.31 us
  transfers between devices with their start and end apart: 2, of which 2 were waited for; matrix products, arithmetic and copies ran while one was open for 7% of the time, Pallas kernels for 0%

commit v1 on v0

v1 whole, which is shorter than its diff:
```python
import functools

import jax
import jax.numpy as jnp
from jax import lax
from jax.experimental import pallas as pl
from jax.experimental.pallas import tpu as pltpu
from jax.sharding import PartitionSpec as P

HEADS = 8
TOK = 128
LAT = 512
KD = 576
ROWS = HEADS * TOK
CHIPS = 8
KEYS = CHIPS * 2 * TOK
SCALE = 192.0**-0.5
LOG2E = 1.4426950408889634
MASKED = -1.0e30
MESH = pl.DeviceIdType.MESH

HALF = KD // 2
A_PIECE = 80
A_ROWS = 4 * A_PIECE
B_ROWS = KD - A_ROWS
B_PIECE = B_ROWS // 8

NN = (((1,), (0,)), ((), ()))
NT = (((1,), (1,)), ((), ()))

A_ORDER = (0, 1, 3, 4, 2, 5, 7, 6)
B_ORDER = (6, 5, 7, 2, 4, 1, 3, 0)
C_TILE = 256


def back(i):
    return (i // 4) * 4 + (4 - i % 4) % 4


def dot(a, b, dims):
    return lax.dot_general(a, b, dims, preferred_element_type=jnp.float32)


def kernel(
    order_ref, q_hbm, k_hbm, g_hbm,
    at_hbm, qg_hbm, kg_hbm,
    q_in, k_in, g_in, q_s, g_s, q_t, g_t, k_t,
    score, dprob, top, total, weighted, lse, delta, prob_b, dscore,
    mine, csend, crecv, chip, arecv, asum, a2recv, a3, a3recv,
    brecv, bsum, b2recv, b3, b3recv, out_t, at_v, qg_v, kg_v,
    in_sem, out_sem,
    k_send, k_recv, y_send, y_recv, f_send, f_recv,
    c_ssem, c_rsem, a1_ssem, a1_rsem, a2_ssem, a2_rsem, a3_ssem, a3_rsem,
    b1_ssem, b1_rsem, b2_ssem, b2_rsem, b3_ssem, b3_rsem,
):
    f32, bf16 = jnp.float32, jnp.bfloat16
    ctx, head = lax.axis_index("ctx"), lax.axis_index("head")
    core = lax.rem(ctx, 2)
    z = lax.rem(ctx // 2, 4)
    y_lo = ctx // 8
    x, y_hi = head // 2, lax.rem(head, 2)

    def chip_of(i, other=0):
        yy = lax.rem(y_lo + i // 4, 2)
        zz = lax.rem(z + i % 4, 4)
        cc = lax.rem(core + other, 2)
        return (yy * 4 + zz) * 2 + cc

    def on_ctx(i):
        return (chip_of(i), head)

    def head_of(k):
        return lax.rem(x + k // 2, 4) * 2 + lax.rem(y_hi + k % 2, 2)

    def on_head(k):
        return (ctx, head_of(k))

    peer = (chip_of(0, 1), head)

    def y_neighbour(step):
        y = lax.rem(y_hi * 2 + y_lo + step, 4)
        return ((lax.rem(y, 2) * 4 + z) * 2 + core, x * 2 + y // 2)

    y_next = (y_neighbour(1), y_neighbour(3))

    load_k = pltpu.make_async_copy(k_hbm, k_in, in_sem.at[0])
    load_q = pltpu.make_async_copy(q_hbm, q_in, in_sem.at[1])
    load_g = pltpu.make_async_copy(g_hbm, g_in, in_sem.at[2])
    load_k.start()
    load_q.start()
    load_g.start()

    barrier = pltpu.get_barrier_semaphore()
    others = [peer] + [on_ctx(i) for i in range(1, 8)] + [on_head(k) for k in range(1, 8)]
    others += [y_next[0], y_next[1]]
    for other in others:
        pl.semaphore_signal(barrier, inc=1, device_id=other, device_id_type=MESH)

    load_k.wait()
    k_t[:, 0:TOK] = k_in[...].T

    def slot(i, u):
        return pl.ds((2 * i + u) * TOK, TOK)

    def send(src, dst, ssem, rsem, device):
        copy = pltpu.make_async_remote_copy(
            src_ref=src, dst_ref=dst, send_sem=ssem, recv_sem=rsem,
            device_id=device, device_id_type=MESH,
        )
        copy.start()
        return copy

    pl.semaphore_wait(barrier, len(others))

    own = k_t.at[:, slot(0, 0)]
    z_copy, y_copy, f_copy = {}, {}, {}
    f_copy[0] = send(own, k_t.at[:, slot(0, 1)], f_send.at[0], f_recv.at[0], peer)
    for i in (1, 3, 2):
        z_copy[back(i)] = send(own, k_t.at[:, slot(back(i), 0)], k_send.at[back(i)], k_recv.at[back(i)], on_ctx(i))

    def across_y(i):
        for n in range(2):
            rows = pl.ds(n * HALF, HALF)
            y_copy[4 + i, n] = send(
                k_t.at[rows, slot(i, 0)], k_t.at[rows, slot(4 + i, 0)],
                y_send.at[i, n], y_recv.at[i, n], y_next[n],
            )

    across_y(0)

    def hand_on(i):
        if i < 4:
            z_copy[i].wait_recv()
            across_y(i)
        else:
            y_copy[i, 0].wait_recv()
            y_copy[i, 1].wait_recv()
        f_copy[i] = send(k_t.at[:, slot(i, 0)], k_t.at[:, slot(i, 1)], f_send.at[i], f_recv.at[i], peer)

    load_q.wait()
    load_g.wait()
    for h in range(HEADS):
        rows = pl.ds(h * TOK, TOK)
        qh = q_in[:, h * KD : (h + 1) * KD]
        q_s[rows, :] = qh
        q_t[:, rows] = (qh.astype(f32) * SCALE).astype(bf16).T
        gh = g_in[:, h * LAT : (h + 1) * LAT]
        g_s[rows, :] = gh
        g_t[:, rows] = gh.T

    top[...] = jnp.full((ROWS, TOK), MASKED, f32)
    total[...] = jnp.zeros((ROWS, TOK), f32)
    weighted[...] = jnp.zeros((ROWS, TOK), f32)
    ahead = lax.broadcasted_iota(jnp.int32, (TOK, TOK), 1) - lax.broadcasted_iota(jnp.int32, (TOK, TOK), 0)
    my_block = order_ref[ctx]

    def scores(i):
        cols = pl.ds(2 * i * TOK, 2 * TOK)
        keys = k_t[:, cols]
        visible = [ahead <= (my_block - order_ref[chip_of(i, u)]) * TOK for u in range(2)]
        for h in range(HEADS):
            rows = pl.ds(h * TOK, TOK)
            sc = dot(q_s[rows, :], keys, NN) * (SCALE * LOG2E)
            dp = dot(g_s[rows, :], keys[:LAT], NN)
            s0 = jnp.where(visible[0], sc[:, :TOK], MASKED)
            s1 = jnp.where(visible[1], sc[:, TOK:], MASKED)
            score[rows, slot(i, 0)] = s0
            score[rows, slot(i, 1)] = s1
            dprob[rows, cols] = dp
            m0 = top[rows, :]
            m1 = jnp.maximum(m0, jnp.maximum(s0, s1))
            shrink = jnp.exp2(m0 - m1)
            e0, e1 = jnp.exp2(s0 - m1), jnp.exp2(s1 - m1)
            top[rows, :] = m1
            total[rows, :] = total[rows, :] * shrink + (e0 + e1)
            weighted[rows, :] = weighted[rows, :] * shrink + (e0 * dp[:, :TOK] + e1 * dp[:, TOK:])

    f_copy[0].wait_recv()
    scores(0)
    hand_on(4)
    hand_on(1)
    hand_on(3)
    f_copy[4].wait_recv()
    scores(4)
    f_copy[1].wait_recv()
    scores(1)
    f_copy[3].wait_recv()
    scores(3)
    hand_on(2)
    f_copy[2].wait_recv()
    scores(2)
    hand_on(5)
    hand_on(7)
    f_copy[5].wait_recv()
    scores(5)
    f_copy[7].wait_recv()
    scores(7)
    hand_on(6)
    f_copy[6].wait_recv()
    scores(6)

    for h in range(HEADS):
        rows = pl.ds(h * TOK, TOK)
        lane_top = top[rows, :]
        row_top = jnp.max(lane_top, axis=1, keepdims=True)
        weight = jnp.exp2(lane_top - row_top)
        row_total = jnp.sum(total[rows, :] * weight, axis=1, keepdims=True)
        row_weighted = jnp.sum(weighted[rows, :] * weight, axis=1, keepdims=True)
        lse[rows, :] = jnp.broadcast_to(row_top + jnp.log2(row_total), (TOK, TOK))
        delta[rows, :] = jnp.broadcast_to(row_weighted / row_total, (TOK, TOK))

    def weights(i):
        for u in range(2):
            cols = slot(i, u)
            p = jnp.exp2(score[:, cols] - lse[...])
            prob_b[:, cols] = p.astype(bf16)
            dscore[:, cols] = (p * (dprob[:, cols] - delta[...])).astype(bf16)

    c_copy, a1_copy, a2_copy, a3_copy = {}, {}, {}, {}
    b1_copy, b2_copy, b3_copy = {}, {}, {}

    def key_grads(i):
        cols = pl.ds(2 * i * TOK, 2 * TOK)
        from_scores = dot(q_t[...], dscore[:, cols], NN)
        from_values = dot(g_t[...], prob_b[:, cols], NN)
        low = from_scores[:LAT] + from_values
        high = from_scores[LAT:]
        mine[i, :LAT, :] = low[:, :TOK]
        mine[i, LAT:, :] = high[:, :TOK]
        csend[i, :LAT, :] = low[:, TOK:].astype(bf16)
        csend[i, LAT:, :] = high[:, TOK:].astype(bf16)

    def to_core(i):
        c_copy[i] = send(csend.at[i], crecv.at[i], c_ssem.at[i], c_rsem.at[i], peer)

    def piece(xx):
        return pl.ds(pl.multiple_of(xx * A_PIECE, 16), A_PIECE)

    def to_links(i):
        c_copy[i].wait_recv()
        chip[i] = (mine[i] + crecv[i].astype(f32)).astype(bf16)
        for dx in (2, 1, 3):
            a1_copy[i, 4 - dx] = send(
                chip.at[i, piece(lax.rem(x + dx, 4))], arecv.at[i, 4 - dx - 1],
                a1_ssem.at[i, 4 - dx - 1], a1_rsem.at[i, 4 - dx - 1], on_head(2 * dx),
            )
        if i:
            j = back(i)
            b1_copy[j] = send(
                chip.at[i, pl.ds(A_ROWS, B_ROWS)], brecv.at[j - 1],
                b1_ssem.at[j - 1], b1_rsem.at[j - 1], on_ctx(i),
            )

    def sum_x(i):
        for dx in (1, 2, 3):
            a1_copy[i, dx].wait_recv()
        part = chip[i, piece(x), :].astype(f32)
        for n in range(3):
            part = part + arecv[i, n].astype(f32)
        asum[i] = part.astype(bf16)
        if i:
            j = back(i)
            a2_copy[j] = send(asum.at[i], a2recv.at[j - 1], a2_ssem.at[j - 1], a2_rsem.at[j - 1], on_ctx(i))

    def back_head(k):
        return ((4 - k // 2) % 4) * 2 + k % 2

    def b_piece(hh):
        return pl.ds(pl.multiple_of(hh * B_PIECE, 16), B_PIECE)

    HEAD_ORDER = (5, 3, 7, 4, 1, 2, 6)

    def b_ctx():
        part = chip[0, A_ROWS:, :].astype(f32)
        for j in range(1, 8):
            b1_copy[j].wait_recv()
            part = part + brecv[j - 1].astype(f32)
        bsum[...] = part.astype(bf16)
        for k in HEAD_ORDER:
            j = back_head(k)
            b2_copy[j] = send(
                bsum.at[b_piece(head_of(k))], b2recv.at[j - 1],
                b2_ssem.at[j - 1], b2_rsem.at[j - 1], on_head(k),
            )

    def a_ctx():
        part = asum[0].astype(f32)
        for j in range(1, 8):
            a2_copy[j].wait_recv()
            part = part + a2recv[j - 1].astype(f32)
        a3[...] = part.astype(bf16)
        for k in HEAD_ORDER:
            j = back_head(k)
            a3_copy[j] = send(a3, a3recv.at[j - 1], a3_ssem.at[j - 1], a3_rsem.at[j - 1], on_head(k))

    def b_head():
        part = bsum[b_piece(head), :].astype(f32)
        for j in range(1, 8):
            b2_copy[j].wait_recv()
            part = part + b2recv[j - 1].astype(f32)
        b3[...] = part.astype(bf16)
        for k in HEAD_ORDER:
            j = back_head(k)
            b3_copy[j] = send(b3, b3recv.at[j - 1], b3_ssem.at[j - 1], b3_rsem.at[j - 1], on_head(k))

    def finish():
        for j in range(1, 8):
            a3_copy[j].wait_recv()
        for dx in range(4):
            first = a3[...] if dx == 0 else a3recv[2 * dx - 1]
            both = first.astype(f32) + a3recv[2 * dx].astype(f32)
            out_t[piece(lax.rem(x + dx, 4)), :] = both.astype(bf16)
        for j in range(8):
            if j:
                b3_copy[j].wait_recv()
            rows = pl.ds(pl.multiple_of(A_ROWS + head_of(j) * B_PIECE, 16), B_PIECE)
            out_t[rows, :] = b3recv[j - 1] if j else b3[...]
        kg_v[...] = out_t[...].T

    at_copy, qg_copy = [], []

    def row_outputs(r):
        rows = pl.ds(r * C_TILE, C_TILE)
        a = dot(prob_b[rows, :], k_t[:LAT, :], NT)
        b = dot(dscore[rows, :], k_t[...], NT) * SCALE
        n = C_TILE // TOK
        for m in range(n):
            h = r * n + m
            at_v[:, h * LAT : (h + 1) * LAT] = a[m * TOK : (m + 1) * TOK].astype(bf16)
            qg_v[:, h * KD : (h + 1) * KD] = b[m * TOK : (m + 1) * TOK].astype(bf16)
        cols = pl.ds(r * n * LAT, n * LAT)
        at_copy.append(pltpu.make_async_copy(at_v.at[:, cols], at_hbm.at[:, cols], out_sem.at[0, r]))
        at_copy[-1].start()
        cols = pl.ds(r * n * KD, n * KD)
        qg_copy.append(pltpu.make_async_copy(qg_v.at[:, cols], qg_hbm.at[:, cols], out_sem.at[1, r]))
        qg_copy[-1].start()

    weights(B_ORDER[0])
    for n, i in enumerate(B_ORDER):
        if n + 1 < CHIPS:
            weights(B_ORDER[n + 1])
        key_grads(i)
        to_core(i)
        if n >= 1:
            to_links(B_ORDER[n - 1])
        if n >= 5:
            sum_x(B_ORDER[n - 5])
    row_outputs(0)
    to_links(B_ORDER[7])
    sum_x(B_ORDER[3])
    sum_x(B_ORDER[4])
    sum_x(B_ORDER[5])
    row_outputs(1)
    sum_x(B_ORDER[6])
    b_ctx()
    row_outputs(2)
    sum_x(B_ORDER[7])
    a_ctx()
    row_outputs(3)
    b_head()
    finish()
    kg_copy = pltpu.make_async_copy(kg_v, kg_hbm, in_sem.at[0])
    kg_copy.start()

    for group in (z_copy, y_copy, f_copy, c_copy, a1_copy, a2_copy, a3_copy, b1_copy, b2_copy, b3_copy):
        for copy in group.values():
            copy.wait_send()
    for copy in at_copy + qg_copy:
        copy.wait()
    kg_copy.wait()


def local(queries, latent_keys, block_order, out_grad):
    f32, bf16 = jnp.float32, jnp.bfloat16
    vmem, dma = pltpu.VMEM, pltpu.SemaphoreType.DMA
    anywhere = pl.BlockSpec(memory_space=pl.ANY)
    scratch = [
        vmem((TOK, HEADS * KD), bf16), vmem((TOK, KD), bf16), vmem((TOK, HEADS * LAT), bf16),
        vmem((ROWS, KD), bf16), vmem((ROWS, LAT), bf16), vmem((KD, ROWS), bf16), vmem((LAT, ROWS), bf16),
        vmem((KD, KEYS), bf16),
        vmem((ROWS, KEYS), f32), vmem((ROWS, KEYS), f32),
        vmem((ROWS, TOK), f32), vmem((ROWS, TOK), f32), vmem((ROWS, TOK), f32),
        vmem((ROWS, TOK), f32), vmem((ROWS, TOK), f32),
        vmem((ROWS, KEYS), bf16), vmem((ROWS, KEYS), bf16),
        vmem((CHIPS, KD, TOK), f32), vmem((CHIPS, KD, TOK), bf16), vmem((CHIPS, KD, TOK), bf16),
        vmem((CHIPS, KD, TOK), bf16),
        vmem((CHIPS, 3, A_PIECE, TOK), bf16), vmem((CHIPS, A_PIECE, TOK), bf16),
        vmem((7, A_PIECE, TOK), bf16), vmem((A_PIECE, TOK), bf16), vmem((7, A_PIECE, TOK), bf16),
        vmem((7, B_ROWS, TOK), bf16), vmem((B_ROWS, TOK), bf16), vmem((7, B_PIECE, TOK), bf16),
        vmem((B_PIECE, TOK), bf16), vmem((7, B_PIECE, TOK), bf16),
        vmem((KD, TOK), bf16),
        vmem((TOK, HEADS * LAT), bf16), vmem((TOK, HEADS * KD), bf16), vmem((TOK, KD), bf16),
        dma((3,)), dma((2, ROWS // C_TILE)),
        dma((4,)), dma((4,)), dma((4, 2)), dma((4, 2)), dma((8,)), dma((8,)),
        dma((8,)), dma((8,)), dma((8, 3)), dma((8, 3)), dma((7,)), dma((7,)), dma((7,)), dma((7,)),
        dma((7,)), dma((7,)), dma((7,)), dma((7,)), dma((7,)), dma((7,)),
    ]
    return pl.pallas_call(
        kernel,
        out_shape=[
            jax.ShapeDtypeStruct((TOK, HEADS * LAT), bf16),
            jax.ShapeDtypeStruct((TOK, HEADS * KD), bf16),
            jax.ShapeDtypeStruct((TOK, KD), bf16),
        ],
        in_specs=[pl.BlockSpec(memory_space=pltpu.SMEM), anywhere, anywhere, anywhere],
        out_specs=[anywhere, anywhere, anywhere],
        scratch_shapes=scratch,
        compiler_params=pltpu.CompilerParams(
            collective_id=0, has_side_effects=True, vmem_limit_bytes=60 * 2**20
        ),
        cost_estimate=pl.CostEstimate(flops=14 * 10**9, bytes_accessed=5 * 10**6, transcendentals=4 * 10**6),
    )(block_order, queries, latent_keys, out_grad)


def solution(mesh):
    return jax.shard_map(
        local,
        mesh=mesh,
        in_specs=(P("ctx", "head"), P("ctx", None), P(), P("ctx", "head")),
        out_specs=(P("ctx", "head"), P("ctx", "head"), P("ctx", None)),
        check_vma=False,
    )
```

time: 197 us -> 63.7 us (0.32)
  waiting for transfers between devices: 97.2 us -> 0 us
  Pallas kernels: 0 us -> 56 us
  blocking collectives: 45.9 us -> 0 us
  matrix products: 26.2 us -> 0 us
  between operations: 14.2 us -> 0.65 us
  local copies, waits for them, and re-layouts: 10.3 us -> 6.81 us
  other arithmetic: 2.6 us -> 0 us
    reduce_scatter x1 -> x0, waiting for transfers between devices: 58.2 us -> none  [local(): lax.psum_scatter(key_accum, 'ctx', scatter_dimension=0, tiled=True)]
    pallas_call x0 -> x1, Pallas kernels: none -> 56 us  [local(): pl.pallas_call(kernel, out_shape=[jax.ShapeDtypeStruct((TOK, HEADS * LAT)...]
    psum x1 -> x0, blocking collectives: 45.9 us -> none  [local(): latent_grad = lax.psum(partial_rows, 'head').astype(jnp.bfloat16)]
    all_gather x1 -> x0, waiting for transfers between devices: 38.2 us -> none  [local(): piece = lax.all_gather(latent_keys, 'ctx', axis=0, tiled=True)]
    dot_general x6 -> x0, matrix products: 26.2 us -> none  [the longest x1 5.59 us: piece_scores(): jnp.einsum('thd,pd->htp', query_three, piece, preferred_element_type=jnp....]
    unnamed x16 -> x5, local copies, waits for them, and re-layouts: 8.29 us -> 5.02 us
    reduce_sum x3 -> x0, other arithmetic: 2.21 us -> none  [the longest x1 2.03 us: local(): new_sum = jnp.sum(weights, axis=2)]
  transfers between devices with their start and end apart: 2 -> 0, of which waited for: 2 -> 0; matrix products, arithmetic and copies ran while one was open for 7% -> 0% of each run, Pallas kernels for 0% -> 0%
where the time goes in v1:
time: 63.7 us; the launch traced here: 63.5 us
  Pallas kernels  56 us (88%)
  local copies, waits for them, and re-layouts  6.81 us (11%)
  between operations  0.65 us (1%)
    pallas_call x1, Pallas kernels, local(): pl.pallas_call(kernel, out_shape=[jax.ShapeDtypeStruct((TOK, HEADS * LAT)...  56 us
    unnamed x5, local copies, waits for them, and re-layouts  5.02 us
    pallas_call x1, local copies, waits for them, and re-layouts, local(): pl.pallas_call(kernel, out_shape=[jax.ShapeDtypeStruct((TOK, HEADS * LAT)...  1.79 us

profile of v1, /device:TPU:0, one launch (start us, length us, event | category | flops | bytes accessed | tf_op | source)
XLA Modules:
  0.0 63.5 jit_solution(14563344966489681796)
XLA Ops:
  0.6 1.7 %copy.7.k_hbm = bf16[128,576]{1,0:T(8,128)(2,1)} copy(bf16[128,576]{0,1:T(8,128)(2,1)} %param.5) | data formatting | bytes 294912 | tf_op args[1]
  2.3 56.0 %shard_map.67 = (bf16[128,4096]{1,0:T(8,128)(2,1)}, bf16[128,4608]{1,0:T(8,128)(2,1)}, bf16[128,576]{1,0:T(8,128)(2,1)}) custom-call(s32[16]{0:T(128)} %order_ref.1, bf16[128,4608]{1,0:T(8,128)(2,1)} %q_hbm.1, bf16[128,576]{1,0:T(8,128)(2,1)} %copy.7.k_hbm, bf16[128,4096]{1,0:T(8,128)(2,1)} %g_hbm.1), custom_call_target="tpu_custom_call" | custom-call | flops 14000000000 | bytes 5000000 | tf_op jit(solution)/shard_map/pallas_call | solution.py:398
  58.4 0.0 copy-start
  58.4 1.8 %copy.8 = bf16[128,576]{0,1:T(8,128)(2,1)} copy(bf16[128,576]{1,0:T(8,128)(2,1)} %get-tuple-element.5) | data formatting | bytes 294912 | tf_op jit(solution)/shard_map/pallas_call | solution.py:398
  60.2 2.3 %copy.11 = bf16[128,4096]{1,0:T(8,128)(2,1)} copy(bf16[128,4096]{1,0:T(8,128)(2,1)} %get-tuple-element.9) | data formatting | bytes 2097152
  62.5 0.0 copy-done
  62.5 1.0 %copy.12 = bf16[128,4608]{1,0:T(8,128)(2,1)} copy(bf16[128,4608]{1,0:T(8,128)(2,1)S(1)} %copy-done) | data formatting | bytes 2359296
Async XLA Ops:
  58.4 4.1 %copy-start = (bf16[128,4608]{1,0:T(8,128)(2,1)S(1)}, bf16[128,4608]{1,0:T(8,128)(2,1)}, u32[]{:S(2)}) copy-start(bf16[128,4608]{1,0:T(8,128)(2,1)} %get-tuple-element.10) | copy-start | bytes 3538948

commit v2 on v1

--- a/solution.py
+++ b/solution.py
@@ -18,8 +18,10 @@
 LOG2E = 1.4426950408889634
 MASKED = -1.0e30
 MESH = pl.DeviceIdType.MESH
-
-HALF = KD // 2
+SPLIT = 4
+
+PARTS = 4
+PART = KD // PARTS
 A_PIECE = 80
 A_ROWS = 4 * A_PIECE
 B_ROWS = KD - A_ROWS
@@ -30,7 +32,6 @@
 
 A_ORDER = (0, 1, 3, 4, 2, 5, 7, 6)
 B_ORDER = (6, 5, 7, 2, 4, 1, 3, 0)
-C_TILE = 256
 
 
 def back(i):
@@ -44,12 +45,12 @@
 def kernel(
     order_ref, q_hbm, k_hbm, g_hbm,
     at_hbm, qg_hbm, kg_hbm,
-    q_in, k_in, g_in, q_s, g_s, q_t, g_t, k_t,
+    q_in, g_in, q_s, g_s, q_t, g_t, k_t,
     score, dprob, top, total, weighted, lse, delta, prob_b, dscore,
     mine, csend, crecv, chip, arecv, asum, a2recv, a3, a3recv,
-    brecv, bsum, b2recv, b3, b3recv, out_t, at_v, qg_v, kg_v,
+    brecv, bsum, b2recv, b3, b3recv, out_t, at_v, qg_v,
     in_sem, out_sem,
-    k_send, k_recv, y_send, y_recv, f_send, f_recv,
+    z_send, z_recv, y_send, y_recv, q_send, q_recv, x_send, x_recv, f_send, f_recv,
     c_ssem, c_rsem, a1_ssem, a1_rsem, a2_ssem, a2_rsem, a3_ssem, a3_rsem,
     b1_ssem, b1_rsem, b2_ssem, b2_rsem, b3_ssem, b3_rsem,
 ):
@@ -83,7 +84,7 @@
 
     y_next = (y_neighbour(1), y_neighbour(3))
 
-    load_k = pltpu.make_async_copy(k_hbm, k_in, in_sem.at[0])
+    load_k = pltpu.make_async_copy(k_hbm, k_t.at[0], in_sem.at[0])
     load_q = pltpu.make_async_copy(q_hbm, q_in, in_sem.at[1])
     load_g = pltpu.make_async_copy(g_hbm, g_in, in_sem.at[2])
     load_k.start()
@@ -91,16 +92,15 @@
     load_g.start()
 
     barrier = pltpu.get_barrier_semaphore()
-    others = [peer] + [on_ctx(i) for i in range(1, 8)] + [on_head(k) for k in range(1, 8)]
-    others += [y_next[0], y_next[1]]
+    others = [peer, y_next[0], y_next[1]] + [on_ctx(i) for i in (1, 3, 2, 6)] + [on_head(k) for k in (2, 6, 4)]
     for other in others:
         pl.semaphore_signal(barrier, inc=1, device_id=other, device_id_type=MESH)
 
-    load_k.wait()
-    k_t[:, 0:TOK] = k_in[...].T
-
     def slot(i, u):
         return pl.ds((2 * i + u) * TOK, TOK)
+
+    def keys_at(i, u=0):
+        return k_t.at[2 * i + u]
 
     def send(src, dst, ssem, rsem, device):
         copy = pltpu.make_async_remote_copy(
@@ -112,30 +112,61 @@
 
     pl.semaphore_wait(barrier, len(others))
 
-    own = k_t.at[:, slot(0, 0)]
-    z_copy, y_copy, f_copy = {}, {}, {}
-    f_copy[0] = send(own, k_t.at[:, slot(0, 1)], f_send.at[0], f_recv.at[0], peer)
-    for i in (1, 3, 2):
-        z_copy[back(i)] = send(own, k_t.at[:, slot(back(i), 0)], k_send.at[back(i)], k_recv.at[back(i)], on_ctx(i))
-
-    def across_y(i):
-        for n in range(2):
-            rows = pl.ds(n * HALF, HALF)
-            y_copy[4 + i, n] = send(
-                k_t.at[rows, slot(i, 0)], k_t.at[rows, slot(4 + i, 0)],
-                y_send.at[i, n], y_recv.at[i, n], y_next[n],
+    def part_of(j, c):
+        return k_t.at[j, pl.ds(c * PART, PART)]
+
+    quarter = pl.ds(pl.multiple_of(x * PART, 16), PART)
+    z_copy, y_copy, q_copy, x_copy, f_copy = {}, {}, {}, {}, {}
+
+    def along_z(i, c):
+        j = back(i)
+        z_copy[j, c] = send(
+            k_hbm.at[pl.ds(c * PART, PART)], part_of(2 * j, c), z_send.at[j, c], z_recv.at[j, c], on_ctx(i)
+        )
+
+    def across_y(i, c):
+        src = part_of(2 * i, c) if i else k_hbm.at[pl.ds(c * PART, PART)]
+        y_copy[4 + i, c] = send(src, part_of(2 * (4 + i), c), y_send.at[i, c], y_recv.at[i, c], y_next[c % 2])
+
+    def fetch(i):
+        q_copy[i] = send(
+            k_hbm.at[quarter], k_t.at[2 * i, quarter], q_send.at[i // 4], q_recv.at[i // 4], on_ctx(i)
+        )
+
+    def along_x(i):
+        q_copy[i].wait_recv()
+        for dx in (2, 1, 3):
+            n = 3 - dx
+            x_copy[i, n] = send(
+                k_t.at[2 * i, quarter], k_t.at[2 * i, quarter],
+                x_send.at[i // 4, n], x_recv.at[i // 4, n], on_head(2 * dx),
             )
 
-    across_y(0)
-
-    def hand_on(i):
-        if i < 4:
-            z_copy[i].wait_recv()
-            across_y(i)
-        else:
-            y_copy[i, 0].wait_recv()
-            y_copy[i, 1].wait_recv()
-        f_copy[i] = send(k_t.at[:, slot(i, 0)], k_t.at[:, slot(i, 1)], f_send.at[i], f_recv.at[i], peer)
+    def to_other(i):
+        src = keys_at(i) if i else k_hbm
+        f_copy[i] = send(src, keys_at(i, 1), f_send.at[i], f_recv.at[i], peer)
+
+    def from_z(i, c):
+        z_copy[i, c].wait_recv()
+        across_y(i, c)
+
+    def from_y(i):
+        for c in range(PARTS):
+            y_copy[i, c].wait_recv()
+        to_other(i)
+
+    def from_x(i):
+        for n in range(3):
+            x_copy[i, n].wait_recv()
+        to_other(i)
+
+    fetch(6)
+    fetch(2)
+    for c in range(PARTS):
+        along_z(1, c)
+        along_z(3, c)
+        across_y(0, c)
+    to_other(0)
 
     load_q.wait()
     load_g.wait()
@@ -156,7 +187,7 @@
 
     def scores(i):
         cols = pl.ds(2 * i * TOK, 2 * TOK)
-        keys = k_t[:, cols]
+        keys = jnp.concatenate([k_t[2 * i], k_t[2 * i + 1]], axis=1)
         visible = [ahead <= (my_block - order_ref[chip_of(i, u)]) * TOK for u in range(2)]
         for h in range(HEADS):
             rows = pl.ds(h * TOK, TOK)
@@ -175,29 +206,30 @@
             total[rows, :] = total[rows, :] * shrink + (e0 + e1)
             weighted[rows, :] = weighted[rows, :] * shrink + (e0 * dp[:, :TOK] + e1 * dp[:, TOK:])
 
+    load_k.wait()
     f_copy[0].wait_recv()
     scores(0)
-    hand_on(4)
-    hand_on(1)
-    hand_on(3)
-    f_copy[4].wait_recv()
-    scores(4)
-    f_copy[1].wait_recv()
-    scores(1)
-    f_copy[3].wait_recv()
-    scores(3)
-    hand_on(2)
-    f_copy[2].wait_recv()
-    scores(2)
-    hand_on(5)
-    hand_on(7)
-    f_copy[5].wait_recv()
-    scores(5)
-    f_copy[7].wait_recv()
-    scores(7)
-    hand_on(6)
-    f_copy[6].wait_recv()
-    scores(6)
+    along_x(2)
+    along_x(6)
+    for c in range(PARTS):
+        from_z(1, c)
+        from_z(3, c)
+    to_other(1)
+    to_other(3)
+    from_y(4)
+    for i in (1, 3, 4):
+        f_copy[i].wait_recv()
+        scores(i)
+    from_x(2)
+    from_x(6)
+    for i in (2, 6):
+        f_copy[i].wait_recv()
+        scores(i)
+    from_y(5)
+    from_y(7)
+    for i in (5, 7):
+        f_copy[i].wait_recv()
+        scores(i)
 
     for h in range(HEADS):
         rows = pl.ds(h * TOK, TOK)
@@ -315,59 +347,88 @@
                 b3_copy[j].wait_recv()
             rows = pl.ds(pl.multiple_of(A_ROWS + head_of(j) * B_PIECE, 16), B_PIECE)
             out_t[rows, :] = b3recv[j - 1] if j else b3[...]
-        kg_v[...] = out_t[...].T
-
-    at_copy, qg_copy = [], []
-
-    def row_outputs(r):
-        rows = pl.ds(r * C_TILE, C_TILE)
-        a = dot(prob_b[rows, :], k_t[:LAT, :], NT)
-        b = dot(dscore[rows, :], k_t[...], NT) * SCALE
-        n = C_TILE // TOK
-        for m in range(n):
-            h = r * n + m
-            at_v[:, h * LAT : (h + 1) * LAT] = a[m * TOK : (m + 1) * TOK].astype(bf16)
-            qg_v[:, h * KD : (h + 1) * KD] = b[m * TOK : (m + 1) * TOK].astype(bf16)
-        cols = pl.ds(r * n * LAT, n * LAT)
-        at_copy.append(pltpu.make_async_copy(at_v.at[:, cols], at_hbm.at[:, cols], out_sem.at[0, r]))
-        at_copy[-1].start()
-        cols = pl.ds(r * n * KD, n * KD)
-        qg_copy.append(pltpu.make_async_copy(qg_v.at[:, cols], qg_hbm.at[:, cols], out_sem.at[1, r]))
-        qg_copy[-1].start()
-
-    weights(B_ORDER[0])
-    for n, i in enumerate(B_ORDER):
-        if n + 1 < CHIPS:
-            weights(B_ORDER[n + 1])
-        key_grads(i)
-        to_core(i)
+
+    out_copy = []
+
+    def row_outputs(n):
+        if n < 2:
+            left, wide, out, first = prob_b, LAT, at_v, n * 256
+        else:
+            left, wide, out, first = dscore, KD, qg_v, (n - 2) * 256
+        size = min(256, wide - first)
+        keys = jnp.concatenate([k_t[j, first : first + size, :] for j in range(2 * CHIPS)], axis=1)
+        part = dot(left[...], keys, NT)
+        if n >= 2:
+            part = part * SCALE
+        for h in range(HEADS):
+            out[:, h * wide + first : h * wide + first + size] = part[h * TOK : (h + 1) * TOK].astype(bf16)
+        if n == 1:
+            out_copy.append(pltpu.make_async_copy(at_v, at_hbm, out_sem.at[0]))
+            out_copy[-1].start()
+        if n == 4:
+            out_copy.append(pltpu.make_async_copy(qg_v, qg_hbm, out_sem.at[1]))
+            out_copy[-1].start()
+
+    groups = [B_ORDER[n : n + 2] for n in range(0, CHIPS, 2)]
+    for i in groups[0]:
+        weights(i)
+    for n, group in enumerate(groups):
+        if n + 1 < len(groups):
+            for i in groups[n + 1]:
+                weights(i)
+        for i in group:
+            key_grads(i)
+        for i in group:
+            to_core(i)
         if n >= 1:
-            to_links(B_ORDER[n - 1])
-        if n >= 5:
-            sum_x(B_ORDER[n - 5])
+            for i in groups[n - 1]:
+                to_links(i)
     row_outputs(0)
-    to_links(B_ORDER[7])
+    for i in groups[3]:
+        to_links(i)
+    sum_x(B_ORDER[0])
+    sum_x(B_ORDER[1])
+    sum_x(B_ORDER[2])
     sum_x(B_ORDER[3])
+    row_outputs(1)
+    row_outputs(2)
     sum_x(B_ORDER[4])
     sum_x(B_ORDER[5])
-    row_outputs(1)
     sum_x(B_ORDER[6])
+    sum_x(B_ORDER[7])
     b_ctx()
-    row_outputs(2)
-    sum_x(B_ORDER[7])
+    row_outputs(3)
     a_ctx()
-    row_outputs(3)
     b_head()
+    row_outputs(4)
     finish()
-    kg_copy = pltpu.make_async_copy(kg_v, kg_hbm, in_sem.at[0])
+    kg_copy = pltpu.make_async_copy(out_t, kg_hbm, in_sem.at[0])
     kg_copy.start()
 
-    for group in (z_copy, y_copy, f_copy, c_copy, a1_copy, a2_copy, a3_copy, b1_copy, b2_copy, b3_copy):
+    for group in (z_copy, y_copy, q_copy, x_copy, f_copy, c_copy, a1_copy, a2_copy, a3_copy, b1_copy, b2_copy, b3_copy):
         for copy in group.values():
             copy.wait_send()
-    for copy in at_copy + qg_copy:
+    for copy in out_copy:
         copy.wait()
     kg_copy.wait()
+
+
+def place(*refs):
+    srcs, dsts, held, sems = refs[:3], refs[3:6], refs[6:9], refs[9]
+    copies = []
+    for n in range(3):
+        rows = srcs[n].shape[0] // SPLIT
+        for c in range(SPLIT):
+            part = pl.ds(c * rows, rows)
+            into = pltpu.make_async_copy(srcs[n].at[part], held[n].at[part], sems.at[0, n, c])
+            out = pltpu.make_async_copy(held[n].at[part], dsts[n].at[part], sems.at[1, n, c])
+            into.start()
+            copies.append((into, out))
+    for into, out in copies:
+        into.wait()
+        out.start()
+    for into, out in copies:
+        out.wait()
 
 
 def local(queries, latent_keys, block_order, out_grad):
@@ -375,9 +436,9 @@
     vmem, dma = pltpu.VMEM, pltpu.SemaphoreType.DMA
     anywhere = pl.BlockSpec(memory_space=pl.ANY)
     scratch = [
-        vmem((TOK, HEADS * KD), bf16), vmem((TOK, KD), bf16), vmem((TOK, HEADS * LAT), bf16),
+        vmem((TOK, HEADS * KD), bf16), vmem((TOK, HEADS * LAT), bf16),
         vmem((ROWS, KD), bf16), vmem((ROWS, LAT), bf16), vmem((KD, ROWS), bf16), vmem((LAT, ROWS), bf16),
-        vmem((KD, KEYS), bf16),
+        vmem((2 * CHIPS, KD, TOK), bf16),
         vmem((ROWS, KEYS), f32), vmem((ROWS, KEYS), f32),
         vmem((ROWS, TOK), f32), vmem((ROWS, TOK), f32), vmem((ROWS, TOK), f32),
         vmem((ROWS, TOK), f32), vmem((ROWS, TOK), f32),
@@ -389,18 +450,19 @@
         vmem((7, B_ROWS, TOK), bf16), vmem((B_ROWS, TOK), bf16), vmem((7, B_PIECE, TOK), bf16),
         vmem((B_PIECE, TOK), bf16), vmem((7, B_PIECE, TOK), bf16),
         vmem((KD, TOK), bf16),
-        vmem((TOK, HEADS * LAT), bf16), vmem((TOK, HEADS * KD), bf16), vmem((TOK, KD), bf16),
-        dma((3,)), dma((2, ROWS // C_TILE)),
-        dma((4,)), dma((4,)), dma((4, 2)), dma((4, 2)), dma((8,)), dma((8,)),
+        vmem((TOK, HEADS * LAT), bf16), vmem((TOK, HEADS * KD), bf16),
+        dma((3,)), dma((2,)),
+        dma((4, PARTS)), dma((4, PARTS)), dma((4, PARTS)), dma((4, PARTS)), dma((2,)), dma((2,)), dma((2, 3)), dma((2, 3)),
+        dma((8,)), dma((8,)),
         dma((8,)), dma((8,)), dma((8, 3)), dma((8, 3)), dma((7,)), dma((7,)), dma((7,)), dma((7,)),
         dma((7,)), dma((7,)), dma((7,)), dma((7,)), dma((7,)), dma((7,)),
     ]
-    return pl.pallas_call(
+    attended, query_grad, key_grad = pl.pallas_call(
         kernel,
         out_shape=[
             jax.ShapeDtypeStruct((TOK, HEADS * LAT), bf16),
             jax.ShapeDtypeStruct((TOK, HEADS * KD), bf16),
-            jax.ShapeDtypeStruct((TOK, KD), bf16),
+            jax.ShapeDtypeStruct((KD, TOK), bf16),
         ],
         in_specs=[pl.BlockSpec(memory_space=pltpu.SMEM), anywhere, anywhere, anywhere],
         out_specs=[anywhere, anywhere, anywhere],
@@ -409,7 +471,16 @@
             collective_id=0, has_side_effects=True, vmem_limit_bytes=60 * 2**20
         ),
         cost_estimate=pl.CostEstimate(flops=14 * 10**9, bytes_accessed=5 * 10**6, transcendentals=4 * 10**6),
-    )(block_order, queries, latent_keys, out_grad)
+    )(block_order, queries, latent_keys.T, out_grad)
+    results = (attended, query_grad, key_grad)
+    attended, query_grad, key_grad = pl.pallas_call(
+        place,
+        out_shape=[jax.ShapeDtypeStruct(r.shape, r.dtype) for r in results],
+        in_specs=[anywhere] * 3,
+        out_specs=[anywhere] * 3,
+        scratch_shapes=[vmem(r.shape, r.dtype) for r in results] + [dma((2, 3, SPLIT))],
+    )(*results)
+    return attended, query_grad, key_grad.T
 
 
 def solution(mesh):

time: 63.7 us -> 53.6 us (0.84)
  local copies, waits for them, and re-layouts: 6.81 us -> 0 us
  Pallas kernels: 56 us -> 52.6 us
    pallas_call x1, Pallas kernels: 56 us -> 50 us  [local(): pl.pallas_call(kernel, out_shape=[jax.ShapeDtypeStruct((TOK, HEADS * LAT)...]
    unnamed x5 -> x0, local copies, waits for them, and re-layouts: 5.02 us -> none
    pallas_call x0 -> x1, Pallas kernels: none -> 2.55 us  [local(): pl.pallas_call(place, out_shape=[jax.ShapeDtypeStruct(r.shape, r.dtype) f...]
    pallas_call x1 -> x0, local copies, waits for them, and re-layouts: 1.79 us -> none  [local(): pl.pallas_call(kernel, out_shape=[jax.ShapeDtypeStruct((TOK, HEADS * LAT)...]
where the time goes in v2:
time: 53.6 us; the launch traced here: 53.4 us
  Pallas kernels  52.6 us (98%)
  between operations  0.8 us (1%)
    pallas_call x1, Pallas kernels, local(): pl.pallas_call(kernel, out_shape=[jax.ShapeDtypeStruct((TOK, HEADS * LAT)...  50 us
    pallas_call x1, Pallas kernels, local(): pl.pallas_call(place, out_shape=[jax.ShapeDtypeStruct(r.shape, r.dtype) f...  2.55 us

profile of v2, /device:TPU:0, one launch (start us, length us, event | category | flops | bytes accessed | tf_op | source)
XLA Modules:
  0.0 53.4 jit_solution(17707572675929300858)
XLA Ops:
  0.6 50.0 %shard_map.67 = (bf16[128,4096]{1,0:T(8,128)(2,1)}, bf16[128,4608]{1,0:T(8,128)(2,1)}, bf16[576,128]{1,0:T(8,128)(2,1)}) custom-call(s32[16]{0:T(128)} %order_ref.1, bf16[128,4608]{1,0:T(8,128)(2,1)} %q_hbm.1, bf16[576,128]{1,0:T(8,128)(2,1)} %bitcast.2, bf16[128,4096]{1,0:T(8,128)(2,1)} %g_hbm.1), custom_call_target="tpu_custom_call" | custom-call | flops 14000000000 | bytes 5000000 | tf_op jit(solution)/shard_map/pallas_call | solution.py:460
  50.7 2.5 %shard_map.68 = (bf16[128,4096]{1,0:T(8,128)(2,1)}, bf16[128,4608]{1,0:T(8,128)(2,1)}, bf16[576,128]{1,0:T(8,128)(2,1)}) custom-call(bf16[128,4096]{1,0:T(8,128)(2,1)} %get-tuple-element.9.refs_0_, bf16[128,4608]{1,0:T(8,128)(2,1)} %get-tuple-element.10.refs_1_, bf16[576,128]{1,0:T(8,128)(2,1)} %get-tuple-element.11.refs_2_), custom_call_target="tpu_custom_call" | custom-call | tf_op jit(solution)/shard_map/pallas_call | solution.py:476

commit v3 on v2

--- a/solution.py
+++ b/solution.py
@@ -30,7 +30,6 @@
 NN = (((1,), (0,)), ((), ()))
 NT = (((1,), (1,)), ((), ()))
 
-A_ORDER = (0, 1, 3, 4, 2, 5, 7, 6)
 B_ORDER = (6, 5, 7, 2, 4, 1, 3, 0)
 
 
@@ -185,19 +184,20 @@
     ahead = lax.broadcasted_iota(jnp.int32, (TOK, TOK), 1) - lax.broadcasted_iota(jnp.int32, (TOK, TOK), 0)
     my_block = order_ref[ctx]
 
-    def scores(i):
-        cols = pl.ds(2 * i * TOK, 2 * TOK)
-        keys = jnp.concatenate([k_t[2 * i], k_t[2 * i + 1]], axis=1)
-        visible = [ahead <= (my_block - order_ref[chip_of(i, u)]) * TOK for u in range(2)]
+    def scores(first, second):
+        pair = (first, second)
+        keys = jnp.concatenate([k_t[2 * i + u] for i, u in pair], axis=1)
+        visible = [ahead <= (my_block - order_ref[chip_of(i, u)]) * TOK for i, u in pair]
         for h in range(HEADS):
             rows = pl.ds(h * TOK, TOK)
             sc = dot(q_s[rows, :], keys, NN) * (SCALE * LOG2E)
             dp = dot(g_s[rows, :], keys[:LAT], NN)
             s0 = jnp.where(visible[0], sc[:, :TOK], MASKED)
             s1 = jnp.where(visible[1], sc[:, TOK:], MASKED)
-            score[rows, slot(i, 0)] = s0
-            score[rows, slot(i, 1)] = s1
-            dprob[rows, cols] = dp
+            score[rows, slot(*first)] = s0
+            score[rows, slot(*second)] = s1
+            dprob[rows, slot(*first)] = dp[:, :TOK]
+            dprob[rows, slot(*second)] = dp[:, TOK:]
             m0 = top[rows, :]
             m1 = jnp.maximum(m0, jnp.maximum(s0, s1))
             shrink = jnp.exp2(m0 - m1)
@@ -208,7 +208,7 @@
 
     load_k.wait()
     f_copy[0].wait_recv()
-    scores(0)
+    scores((0, 0), (0, 1))
     along_x(2)
     along_x(6)
     for c in range(PARTS):
@@ -216,20 +216,25 @@
         from_z(3, c)
     to_other(1)
     to_other(3)
+    scores((1, 0), (3, 0))
     from_y(4)
-    for i in (1, 3, 4):
-        f_copy[i].wait_recv()
-        scores(i)
+    f_copy[1].wait_recv()
+    f_copy[3].wait_recv()
+    scores((1, 1), (3, 1))
+    f_copy[4].wait_recv()
+    scores((4, 0), (4, 1))
     from_x(2)
     from_x(6)
-    for i in (2, 6):
-        f_copy[i].wait_recv()
-        scores(i)
+    scores((2, 0), (6, 0))
     from_y(5)
     from_y(7)
-    for i in (5, 7):
-        f_copy[i].wait_recv()
-        scores(i)
+    scores((5, 0), (7, 0))
+    f_copy[2].wait_recv()
+    f_copy[6].wait_recv()
+    scores((2, 1), (6, 1))
+    f_copy[5].wait_recv()
+    f_copy[7].wait_recv()
+    scores((5, 1), (7, 1))
 
     for h in range(HEADS):
         rows = pl.ds(h * TOK, TOK)

time: 53.6 us -> 51.1 us (0.953)
  Pallas kernels: 52.6 us -> 49.9 us
    pallas_call x1, Pallas kernels: 50 us -> 47.4 us  [local(): pl.pallas_call(kernel, out_shape=[jax.ShapeDtypeStruct((TOK, HEADS * LAT)...]
where the time goes in v3:
time: 51.1 us; the launch traced here: 50.7 us
  Pallas kernels  49.9 us (98%)
  between operations  0.8 us (2%)
    pallas_call x1, Pallas kernels, local(): pl.pallas_call(kernel, out_shape=[jax.ShapeDtypeStruct((TOK, HEADS * LAT)...  47.4 us
    pallas_call x1, Pallas kernels, local(): pl.pallas_call(place, out_shape=[jax.ShapeDtypeStruct(r.shape, r.dtype) f...  2.55 us

profile of v3, /device:TPU:0, one launch (start us, length us, event | category | flops | bytes accessed | tf_op | source)
XLA Modules:
  0.0 50.7 jit_solution(2387128940807061727)
XLA Ops:
  0.6 47.4 %shard_map.67 = (bf16[128,4096]{1,0:T(8,128)(2,1)}, bf16[128,4608]{1,0:T(8,128)(2,1)}, bf16[576,128]{1,0:T(8,128)(2,1)}) custom-call(s32[16]{0:T(128)} %order_ref.1, bf16[128,4608]{1,0:T(8,128)(2,1)} %q_hbm.1, bf16[576,128]{1,0:T(8,128)(2,1)} %bitcast.2, bf16[128,4096]{1,0:T(8,128)(2,1)} %g_hbm.1), custom_call_target="tpu_custom_call" | custom-call | flops 14000000000 | bytes 5000000 | tf_op jit(solution)/shard_map/pallas_call | solution.py:465
  48.0 2.5 %shard_map.68 = (bf16[128,4096]{1,0:T(8,128)(2,1)}, bf16[128,4608]{1,0:T(8,128)(2,1)}, bf16[576,128]{1,0:T(8,128)(2,1)}) custom-call(bf16[128,4096]{1,0:T(8,128)(2,1)} %get-tuple-element.9.refs_0_, bf16[128,4608]{1,0:T(8,128)(2,1)} %get-tuple-element.10.refs_1_, bf16[576,128]{1,0:T(8,128)(2,1)} %get-tuple-element.11.refs_2_), custom_call_target="tpu_custom_call" | custom-call | tf_op jit(solution)/shard_map/pallas_call | solution.py:481

commit v4 on v3

--- a/solution.py
+++ b/solution.py
@@ -18,7 +18,6 @@
 LOG2E = 1.4426950408889634
 MASKED = -1.0e30
 MESH = pl.DeviceIdType.MESH
-SPLIT = 4
 
 PARTS = 4
 PART = KD // PARTS
@@ -43,12 +42,12 @@
 
 def kernel(
     order_ref, q_hbm, k_hbm, g_hbm,
-    at_hbm, qg_hbm, kg_hbm,
+    at_v, qg_v, out_t,
     q_in, g_in, q_s, g_s, q_t, g_t, k_t,
     score, dprob, top, total, weighted, lse, delta, prob_b, dscore,
     mine, csend, crecv, chip, arecv, asum, a2recv, a3, a3recv,
-    brecv, bsum, b2recv, b3, b3recv, out_t, at_v, qg_v,
-    in_sem, out_sem,
+    brecv, bsum, b2recv, b3, b3recv,
+    in_sem,
     z_send, z_recv, y_send, y_recv, q_send, q_recv, x_send, x_recv, f_send, f_recv,
     c_ssem, c_rsem, a1_ssem, a1_rsem, a2_ssem, a2_rsem, a3_ssem, a3_rsem,
     b1_ssem, b1_rsem, b2_ssem, b2_rsem, b3_ssem, b3_rsem,
@@ -353,8 +352,6 @@
             rows = pl.ds(pl.multiple_of(A_ROWS + head_of(j) * B_PIECE, 16), B_PIECE)
             out_t[rows, :] = b3recv[j - 1] if j else b3[...]
 
-    out_copy = []
-
     def row_outputs(n):
         if n < 2:
             left, wide, out, first = prob_b, LAT, at_v, n * 256
@@ -367,12 +364,6 @@
             part = part * SCALE
         for h in range(HEADS):
             out[:, h * wide + first : h * wide + first + size] = part[h * TOK : (h + 1) * TOK].astype(bf16)
-        if n == 1:
-            out_copy.append(pltpu.make_async_copy(at_v, at_hbm, out_sem.at[0]))
-            out_copy[-1].start()
-        if n == 4:
-            out_copy.append(pltpu.make_async_copy(qg_v, qg_hbm, out_sem.at[1]))
-            out_copy[-1].start()
 
     groups = [B_ORDER[n : n + 2] for n in range(0, CHIPS, 2)]
     for i in groups[0]:
@@ -407,33 +398,9 @@
     b_head()
     row_outputs(4)
     finish()
-    kg_copy = pltpu.make_async_copy(out_t, kg_hbm, in_sem.at[0])
-    kg_copy.start()
-
     for group in (z_copy, y_copy, q_copy, x_copy, f_copy, c_copy, a1_copy, a2_copy, a3_copy, b1_copy, b2_copy, b3_copy):
         for copy in group.values():
             copy.wait_send()
-    for copy in out_copy:
-        copy.wait()
-    kg_copy.wait()
-
-
-def place(*refs):
-    srcs, dsts, held, sems = refs[:3], refs[3:6], refs[6:9], refs[9]
-    copies = []
-    for n in range(3):
-        rows = srcs[n].shape[0] // SPLIT
-        for c in range(SPLIT):
-            part = pl.ds(c * rows, rows)
-            into = pltpu.make_async_copy(srcs[n].at[part], held[n].at[part], sems.at[0, n, c])
-            out = pltpu.make_async_copy(held[n].at[part], dsts[n].at[part], sems.at[1, n, c])
-            into.start()
-            copies.append((into, out))
-    for into, out in copies:
-        into.wait()
-        out.start()
-    for into, out in copies:
-        out.wait()
 
 
 def local(queries, latent_keys, block_order, out_grad):
@@ -454,9 +421,7 @@
         vmem((7, A_PIECE, TOK), bf16), vmem((A_PIECE, TOK), bf16), vmem((7, A_PIECE, TOK), bf16),
         vmem((7, B_ROWS, TOK), bf16), vmem((B_ROWS, TOK), bf16), vmem((7, B_PIECE, TOK), bf16),
         vmem((B_PIECE, TOK), bf16), vmem((7, B_PIECE, TOK), bf16),
-        vmem((KD, TOK), bf16),
-        vmem((TOK, HEADS * LAT), bf16), vmem((TOK, HEADS * KD), bf16),
-        dma((3,)), dma((2,)),
+        dma((3,)),
         dma((4, PARTS)), dma((4, PARTS)), dma((4, PARTS)), dma((4, PARTS)), dma((2,)), dma((2,)), dma((2, 3)), dma((2, 3)),
         dma((8,)), dma((8,)),
         dma((8,)), dma((8,)), dma((8, 3)), dma((8, 3)), dma((7,)), dma((7,)), dma((7,)), dma((7,)),
@@ -465,26 +430,16 @@
     attended, query_grad, key_grad = pl.pallas_call(
         kernel,
         out_shape=[
-            jax.ShapeDtypeStruct((TOK, HEADS * LAT), bf16),
-            jax.ShapeDtypeStruct((TOK, HEADS * KD), bf16),
-            jax.ShapeDtypeStruct((KD, TOK), bf16),
+            vmem((TOK, HEADS * LAT), bf16), vmem((TOK, HEADS * KD), bf16), vmem((KD, TOK), bf16),
         ],
         in_specs=[pl.BlockSpec(memory_space=pltpu.SMEM), anywhere, anywhere, anywhere],
-        out_specs=[anywhere, anywhere, anywhere],
+        out_specs=[pl.BlockSpec(memory_space=pltpu.VMEM)] * 3,
         scratch_shapes=scratch,
         compiler_params=pltpu.CompilerParams(
             collective_id=0, has_side_effects=True, vmem_limit_bytes=60 * 2**20
         ),
         cost_estimate=pl.CostEstimate(flops=14 * 10**9, bytes_accessed=5 * 10**6, transcendentals=4 * 10**6),
     )(block_order, queries, latent_keys.T, out_grad)
-    results = (attended, query_grad, key_grad)
-    attended, query_grad, key_grad = pl.pallas_call(
-        place,
-        out_shape=[jax.ShapeDtypeStruct(r.shape, r.dtype) for r in results],
-        in_specs=[anywhere] * 3,
-        out_specs=[anywhere] * 3,
-        scratch_shapes=[vmem(r.shape, r.dtype) for r in results] + [dma((2, 3, SPLIT))],
-    )(*results)
     return attended, query_grad, key_grad.T
 
 

time: 51.1 us -> 50.4 us (0.986)
  Pallas kernels: 49.9 us -> 46.8 us
  local copies, waits for them, and re-layouts: 0 us -> 2.65 us
    pallas_call x2 -> x1, Pallas kernels: 49.9 us -> 46.8 us  [local(): pl.pallas_call(kernel, out_shape=[vmem((TOK, HEADS * LAT), bf16), vmem((T...]
    unnamed x0 -> x3, local copies, waits for them, and re-layouts: none -> 2.65 us
where the time goes in v4:
time: 50.4 us; the launch traced here: 50.1 us
  Pallas kernels  46.8 us (93%)
  local copies, waits for them, and re-layouts  2.65 us (5%)
  between operations  0.64 us (1%)
    pallas_call x1, Pallas kernels, local(): pl.pallas_call(kernel, out_shape=[vmem((TOK, HEADS * LAT), bf16), vmem((T...  46.8 us
    unnamed x3, local copies, waits for them, and re-layouts  2.65 us

profile of v4, /device:TPU:0, one launch (start us, length us, event | category | flops | bytes accessed | tf_op | source)
XLA Modules:
  0.0 50.1 jit_solution(17323578845539573215)
XLA Ops:
  0.6 46.8 %shard_map.67 = (bf16[128,4096]{1,0:T(8,128)(2,1)S(1)}, bf16[128,4608]{1,0:T(8,128)(2,1)S(1)}, bf16[576,128]{1,0:T(8,128)(2,1)S(1)}) custom-call(s32[16]{0:T(128)} %order_ref.1, bf16[128,4608]{1,0:T(8,128)(2,1)} %q_hbm.1, bf16[576,128]{1,0:T(8,128)(2,1)} %bitcast.3, bf16[128,4096]{1,0:T(8,128)(2,1)} %g_hbm.1), custom_call_target="tpu_custom_call" | custom-call | flops 14000000000 | bytes 5000000 | tf_op jit(solution)/shard_map/pallas_call | solution.py:430
  47.5 1.0 %copy.10 = bf16[128,4096]{1,0:T(8,128)(2,1)} copy(bf16[128,4096]{1,0:T(8,128)(2,1)S(1)} %get-tuple-element.9) | data formatting | bytes 2097152
  48.4 0.7 %copy.12 = bf16[128,576]{0,1:T(8,128)(2,1)} copy(bf16[128,576]{0,1:T(8,128)(2,1)S(1)} %bitcast.2) | data formatting | bytes 294912
  49.1 1.0 %copy.11 = bf16[128,4608]{1,0:T(8,128)(2,1)} copy(bf16[128,4608]{1,0:T(8,128)(2,1)S(1)} %get-tuple-element.10) | data formatting | bytes 2359296

commit v5 on v4

--- a/solution.py
+++ b/solution.py
@@ -382,20 +382,16 @@
     row_outputs(0)
     for i in groups[3]:
         to_links(i)
-    sum_x(B_ORDER[0])
-    sum_x(B_ORDER[1])
-    sum_x(B_ORDER[2])
-    sum_x(B_ORDER[3])
+    for n in range(0, 4):
+        sum_x(B_ORDER[n])
     row_outputs(1)
+    for n in range(4, 8):
+        sum_x(B_ORDER[n])
+    b_ctx()
     row_outputs(2)
-    sum_x(B_ORDER[4])
-    sum_x(B_ORDER[5])
-    sum_x(B_ORDER[6])
-    sum_x(B_ORDER[7])
-    b_ctx()
-    row_outputs(3)
     a_ctx()
     b_head()
+    row_outputs(3)
     row_outputs(4)
     finish()
     for group in (z_copy, y_copy, q_copy, x_copy, f_copy, c_copy, a1_copy, a2_copy, a3_copy, b1_copy, b2_copy, b3_copy):

time: 50.4 us -> 50.4 us (level)
  no operation moved by 1% of the time
where the time goes in v5:
time: 50.4 us; the launch traced here: 50.1 us
  Pallas kernels  46.8 us (93%)
  local copies, waits for them, and re-layouts  2.65 us (5%)
  between operations  0.64 us (1%)
    pallas_call x1, Pallas kernels, local(): pl.pallas_call(kernel, out_shape=[vmem((TOK, HEADS * LAT), bf16), vmem((T...  46.8 us
    unnamed x3, local copies, waits for them, and re-layouts  2.65 us

profile of v5, /device:TPU:0, one launch (start us, length us, event | category | flops | bytes accessed | tf_op | source)
XLA Modules:
  0.0 50.1 jit_solution(15708421961266563686)
XLA Ops:
  0.6 46.8 %shard_map.67 = (bf16[128,4096]{1,0:T(8,128)(2,1)S(1)}, bf16[128,4608]{1,0:T(8,128)(2,1)S(1)}, bf16[576,128]{1,0:T(8,128)(2,1)S(1)}) custom-call(s32[16]{0:T(128)} %order_ref.1, bf16[128,4608]{1,0:T(8,128)(2,1)} %q_hbm.1, bf16[576,128]{1,0:T(8,128)(2,1)} %bitcast.3, bf16[128,4096]{1,0:T(8,128)(2,1)} %g_hbm.1), custom_call_target="tpu_custom_call" | custom-call | flops 14000000000 | bytes 5000000 | tf_op jit(solution)/shard_map/pallas_call | solution.py:426
  47.5 1.0 %copy.10 = bf16[128,4096]{1,0:T(8,128)(2,1)} copy(bf16[128,4096]{1,0:T(8,128)(2,1)S(1)} %get-tuple-element.9) | data formatting | bytes 2097152
  48.4 0.7 %copy.12 = bf16[128,576]{0,1:T(8,128)(2,1)} copy(bf16[128,576]{0,1:T(8,128)(2,1)S(1)} %bitcast.2) | data formatting | bytes 294912
  49.1 1.0 %copy.11 = bf16[128,4608]{1,0:T(8,128)(2,1)} copy(bf16[128,4608]{1,0:T(8,128)(2,1)S(1)} %get-tuple-element.10) | data formatting | bytes 2359296
